TPU v7x, 256 devices: a whole 4x4x8 slice. The times are simulated.
256 devices in a mesh: seq: 32 (over z, x), head: 8 (over y, core).
Axes of the slice: x: 4, y: 4, z: 8, core: 2. Of those that a mesh axis runs over, the one named last changes fastest.
Arguments:
- query_rows: bfloat16 [24576, 4096], P('seq', 'head'), may hold values from -6 to 6
- key_rows: bfloat16 [24576, 4096], P('seq', 'head'), may hold values from -6 to 6
- value_rows: bfloat16 [24576, 4096], P('seq', 'head'), may hold values from -6 to 6
- grad_out: bfloat16 [24576, 4096], P('seq', 'head'), may hold values from -6 to 6
- doc_lengths: int32 [16], replicated, may hold values from 1 to 13440, as said below
Outputs:
- attended: bfloat16 [24576, 4096], P('seq', 'head')
- grad_query: bfloat16 [24576, 4096], P('seq', 'head')
- grad_key: bfloat16 [24576, 4096], P('seq', 'head')
- grad_value: bfloat16 [24576, 4096], P('seq', 'head')
Inputs may be any that keep to these rules, and one draw needn't show every extreme that they name: `doc_lengths`: the 16 lengths sum to 24576; the last document is the longest, exactly 13440 long, and the first is longer than 768.
All inputs are finite; a program needn't handle non-finite values.
Results may differ from a plain program's by a relative error of at most 0.0043.
Values sent between devices are 32-bit elements; how exact they have to be, the bound alone decides.
A program may use at most 128 MiB of HBM per device.

v0:
```python
import jax
import jax.numpy as jnp
from jax import lax
from jax.sharding import PartitionSpec as P

DH = 128


def prefix(part, axis, combine, identity, reverse):
    count = lax.axis_size(axis)
    place = lax.axis_index(axis)
    ahead = count - 1 - place if reverse else place
    gathered = jax.tree.map(lambda a: lax.all_gather(a, axis), part)
    state = jax.tree.map(lambda a, e: jnp.zeros_like(a) + jnp.asarray(e, a.dtype), part, identity)

    def one(lap, state):
        source = count - 1 - lap if reverse else lap
        return combine(
            state, jax.tree.map(lambda a: lax.dynamic_index_in_dim(a, source, 0, False), gathered)
        )

    return lax.fori_loop(0, ahead, one, state)


def doc_layout(doc_lengths, offset, count):
    starts = jnp.cumsum(doc_lengths, dtype=jnp.int32) - doc_lengths
    positions = offset + jnp.arange(count, dtype=jnp.int32)
    first_start = jnp.max(
        jnp.where(starts[None, :] <= positions[:, None], starts[None, :], 0), axis=1
    )
    counts = (positions - first_start + 1).astype(jnp.float32)
    rowscale = 1.0 / jnp.sqrt(counts * DH)
    order = jnp.arange(count, dtype=jnp.int32)
    same_doc = (first_start[:, None] == first_start[None, :]) & (order[None, :] <= order[:, None])
    head_mask = (first_start < offset).astype(jnp.float32)
    tail_mask = (first_start == first_start[count - 1]).astype(jnp.float32)
    has_start = (first_start[count - 1] >= offset).astype(jnp.float32).reshape(1)
    return (rowscale, same_doc, head_mask, tail_mask, has_start)


def segment_join(earlier, later):
    return (
        jnp.where(later[1] > 0.5, later[0], earlier[0] + later[0]),
        jnp.maximum(earlier[1], later[1]),
    )


def per_device(query_rows, key_rows, value_rows, grad_out, doc_lengths):
    highest = lax.Precision.HIGHEST
    tok_count = query_rows.shape[0]
    head_count = query_rows.shape[1] // DH
    shape3 = (tok_count, head_count, DH)
    query_b = query_rows.reshape(shape3)
    key_b = key_rows.reshape(shape3)
    value_b = value_rows.reshape(shape3)
    grad_b = grad_out.reshape(shape3)
    offset = lax.axis_index("seq") * tok_count
    rowscale, same_doc, head_mask, tail_mask, has_start = doc_layout(doc_lengths, offset, tok_count)
    tail_keys = key_b * tail_mask.astype(jnp.bfloat16)[:, None, None]
    tail_state = jnp.einsum("shi,shj->hij", tail_keys, value_b, preferred_element_type=jnp.float32)
    query_f = query_b.astype(jnp.float32)
    scaled = rowscale[:, None, None] * grad_b.astype(jnp.float32)
    head_grad = jnp.einsum(
        "thi,thj->hij", query_f * head_mask[:, None, None], scaled, precision=highest
    )
    empty = (jnp.zeros_like(tail_state), jnp.zeros((1,), jnp.float32))
    state_in, _ = prefix((tail_state, has_start), "seq", segment_join, empty, False)
    grad_in, _ = prefix((head_grad, has_start), "seq", segment_join, empty, True)
    scores = jnp.einsum("thd,shd->hts", query_b, key_b, preferred_element_type=jnp.float32)
    scores_low = jnp.where(same_doc[None], scores, 0.0).astype(jnp.bfloat16)
    raw_grad = jnp.einsum("thd,shd->hts", grad_b, value_b, preferred_element_type=jnp.float32)
    grad_low = jnp.where(same_doc[None], raw_grad * rowscale[None, :, None], 0.0).astype(
        jnp.bfloat16
    )
    scaled_low = scaled.astype(jnp.bfloat16)
    key_f = key_b.astype(jnp.float32)
    value_f = value_b.astype(jnp.float32)
    carried = jnp.einsum("thi,hij->thj", query_f, state_in, precision=highest)
    attended = rowscale[:, None, None] * (
        jnp.einsum("hts,shd->thd", scores_low, value_b, preferred_element_type=jnp.float32)
        + head_mask[:, None, None] * carried
    )
    grad_query = jnp.einsum(
        "hts,shd->thd", grad_low, key_b, preferred_element_type=jnp.float32
    ) + head_mask[:, None, None] * jnp.einsum("hij,thj->thi", state_in, scaled, precision=highest)
    grad_key = jnp.einsum(
        "hts,thd->shd", grad_low, query_b, preferred_element_type=jnp.float32
    ) + tail_mask[:, None, None] * jnp.einsum("hij,shj->shi", grad_in, value_f, precision=highest)
    grad_value = jnp.einsum(
        "hts,thd->shd", scores_low, scaled_low, preferred_element_type=jnp.float32
    ) + tail_mask[:, None, None] * jnp.einsum("shi,hij->shj", key_f, grad_in, precision=highest)
    flat = (tok_count, head_count * DH)
    return (
        attended.astype(jnp.bfloat16).reshape(flat),
        grad_query.astype(jnp.bfloat16).reshape(flat),
        grad_key.astype(jnp.bfloat16).reshape(flat),
        grad_value.astype(jnp.bfloat16).reshape(flat),
    )


def solution(mesh):
    placed = (P("seq", "head"), P("seq", "head"), P("seq", "head"), P("seq", "head"), P())
    return jax.shard_map(
        per_device,
        mesh=mesh,
        in_specs=placed,
        out_specs=(P("seq", "head"), P("seq", "head"), P("seq", "head"), P("seq", "head")),
        check_vma=False,
    )
```

profile of v0, /device:TPU:230, one launch (start us, length us, event | category | flops | bytes accessed | tf_op | source)
XLA Modules:
  0.0 309.0 jit_solution(332614746718354826)
XLA Ops:
  7.3 0.8 copy.78
  8.3 0.7 sub.24
  9.0 0.6 slice.4
  9.6 0.6 fusion.32
  10.2 1.4 copy.106
  12.0 2.5 fusion.4
  14.5 1.4 copy.133
  15.9 1.1 fusion.15
  17.7 0.6 dynamic-slice
  18.3 0.7 dynamic-update-slice
  19.0 69.9 %all-reduce = f32[32]{0:T(128)S(1)} all-reduce(f32[32]{0:T(128)S(1)} %dynamic-update-slice), channel_id=1, replica_groups=mesh['seq'=32,'head'=8] {'seq'}, use_global_device_ids=true, to_apply=%add | all-reduce | flops 32 | bytes 256
  89.3 2.7 select_convert_fusion.1
  92.1 2.9 fusion.10
  95.0 4.2 %select_convert_fusion = bf16[4,768,768]{2,1,0:T(8,128)(2,1)} fusion(f32[768]{0:T(1024)S(1)} %multiply_rsqrt_fusion, pred[768,768]{1,0:T(8,128)(4,1)S(1)} %fusion, bf16[768,4,128]{0,2,1:T(8,128)(2,1)S(1)} %bitcast.100, bf16[768,512]{1,0:T(8,128)(2,1)S(1)} %copy-done), kind=kOutput, calls=%fused_computation.4 | convolution fusion | flops 611057664 | bytes 6884352 | tf_op jit(solution)/shard_map/thd,shd->hts/dot_general | solution.py:71
  99.2 10.6 %all-gather.7.cloned.1.call-done = f32[128,128,128]{2,1,0:T(8,128)} async-done(((f32[4,128,128]{2,1,0:T(8,128)}), f32[128,128,128]{2,1,0:T(8,128)}) %all-gather.7.cloned.1.call-update) | async-done | bytes 8388624 | tf_op jit(solution)/shard_map/all_gather | solution.py:13
  109.9 0.8 fusion.12
  111.0 2.0 fusion.17
  113.0 95.5 %all-gather.5.cloned.1.call-done = f32[128,128,128]{2,1,0:T(8,128)} async-done(((f32[4,128,128]{2,1,0:T(8,128)}), f32[128,128,128]{2,1,0:T(8,128)}) %all-gather.5.cloned.1.call-update) | async-done | bytes 8388624 | tf_op jit(solution)/shard_map/all_gather | solution.py:13
  208.5 71.6 %while.26 = (s32[]{:T(128)}, f32[4,128,128]{2,1,0:T(8,128)S(1)}, s32[]{:T(128)}, f32[32,1]{0,1:T(1,128)S(1)}, f32[32,4,128,128]{3,2,1,0:T(8,128)}, /*index=5*/s32[]{:T(128)}, s32[]{:T(128)}, s32[]{:T(128)}) while((s32[]{:T(128)}, f32[4,128,128]{2,1,0:T(8,128)S(1)}, s32[]{:T(128)}, f32[32,1]{0,1:T(1,128)S(1)}, f32[32,4,128,128]{3,2,1,0:T(8,128)}, ...), condition=%wide.region_3.4_spmd, body=%wide.region_2.3_spmd.sunk | while | flops 131078 | bytes 786573 | solution.py:22
  209.1 1.7 add_select_fusion.4
  210.8 0.6 fusion.56
  211.4 1.7 add_select_fusion.4
  213.1 0.6 fusion.56
  213.7 1.7 add_select_fusion.4
  215.4 0.6 fusion.56
  216.0 1.7 add_select_fusion.4
  218.3 1.7 add_select_fusion.4
  220.0 0.6 fusion.56
  220.6 1.7 add_select_fusion.4
  222.3 0.6 fusion.56
  222.9 1.7 add_select_fusion.4
  225.2 1.7 add_select_fusion.4
  227.5 1.7 add_select_fusion.4
  229.8 1.7 add_select_fusion.4
  232.1 1.7 add_select_fusion.4
  234.4 1.7 add_select_fusion.4
  236.7 1.7 add_select_fusion.4
  239.0 1.7 add_select_fusion.4
  241.3 1.7 add_select_fusion.4
  243.6 1.7 add_select_fusion.4
  245.9 1.7 add_select_fusion.4
  248.2 1.7 add_select_fusion.4
  250.5 1.7 add_select_fusion.4
  252.8 1.7 add_select_fusion.4
  255.1 1.7 add_select_fusion.4
  257.4 1.7 add_select_fusion.4
  259.7 1.7 add_select_fusion.4
  262.0 1.7 add_select_fusion.4
  264.4 1.7 add_select_fusion.4
  266.7 1.7 add_select_fusion.4
  269.0 1.7 add_select_fusion.4
  271.3 1.7 add_select_fusion.4
  273.6 1.7 add_select_fusion.4
  275.9 1.7 add_select_fusion.4
  278.2 1.7 add_select_fusion.4
  280.1 2.9 fusion.8
  283.0 4.9 %add_convert_fusion.1 = bf16[4,768,128]{1,2,0:T(8,128)(2,1)} fusion(f32[4,768,128]{1,2,0:T(8,128)S(1)} %fusion.8, bf16[4,768,768]{2,1,0:T(8,128)(2,1)} %select_convert_fusion, bf16[768,4,128]{0,2,1:T(8,128)(2,1)S(1)} %bitcast.106, f32[768]{0:T(1024)S(1)} %get-tuple-element.172), kind=kOutput, calls=%fused_computation.17 | convolution fusion | flops 605159424 | bytes 7867392 | tf_op jit(solution)/shard_map/hts,shd->thd/dot_general | solution.py:83
  287.9 1.8 fusion.1
  289.7 2.4 copy.99
  292.1 2.3 copy.98
  294.4 4.4 %add_convert_fusion = bf16[4,128,768]{2,1,0:T(8,128)(2,1)} fusion(f32[4,128,768]{2,1,0:T(8,128)S(1)} %copy-done.2, bf16[4,768,768]{2,1,0:T(8,128)(2,1)} %copy-done.1, bf16[768,4,128]{0,2,1:T(8,128)(2,1)} %bitcast.102, f32[768]{0:T(1024)S(1)} %get-tuple-element.171, f32[768]{0:T(1024)S(1)} %multiply_rsqrt_fusion), kind=kOutput, calls=%fused_computation.13 | convolution fusion | flops 606339072 | bytes 7870464 | tf_op jit(solution)/shard_map/hts,thd->shd/dot_general | solution.py:89
  298.9 1.0 fusion.3
  299.8 1.2 copy.97
  301.0 1.2 copy.100
  (68 shorter events, 16.7 us)
Async XLA Ops:
  7.2 8.8 %copy-start = (bf16[768,512]{1,0:T(8,128)(2,1)S(1)}, bf16[768,512]{1,0:T(8,128)(2,1)}, u32[]{:S(2)}) copy-start(bf16[768,512]{1,0:T(8,128)(2,1)} %param.11) | copy-start | bytes 2359300
  7.2 4.5 %copy-start.9 = (bf16[768,512]{1,0:T(8,128)(2,1)S(1)}, bf16[768,512]{1,0:T(8,128)(2,1)}, u32[]{:S(2)}) copy-start(bf16[768,512]{1,0:T(8,128)(2,1)} %param.12) | copy-start | bytes 2359300
  7.2 102.6 %all-gather.7.cloned.1.call-start = ((), (), s32[]{:S(2)}) async-start(), calls=%async_computation.1 | async-start | bytes 8650752 | tf_op jit(solution)/shard_map/all_gather | solution.py:13
  11.9 83.0 %copy-start.3 = (bf16[768,512]{0,1:T(8,128)(2,1)}, bf16[768,512]{0,1:T(8,128)(2,1)S(1)}, u32[]{:S(2)}) copy-start(bf16[768,512]{0,1:T(8,128)(2,1)S(1)} %copy.86) | copy-start | bytes 2359300
  14.5 194.0 %all-gather.5.cloned.1.call-start = ((), (), s32[]{:S(2)}) async-start(), calls=%async_computation | async-start | bytes 8650752 | tf_op jit(solution)/shard_map/all_gather | solution.py:13
  15.9 73.4 %copy-start.6 = (bf16[768,512]{0,1:T(8,128)(2,1)}, bf16[768,512]{0,1:T(8,128)(2,1)S(1)}, u32[]{:S(2)}) copy-start(bf16[768,512]{0,1:T(8,128)(2,1)S(1)} %copy.133) | copy-start | bytes 2359300
  15.9 1.7 copy-start.10
  92.1 2.9 copy-start.1
  109.9 1.1 copy-start.8
  280.0 2.9 copy-start.7
  280.1 7.9 %slice-start = ((s8[4718592]{0:T(1024)(128)(4,1)}), s8[4194304]{0:T(1024)(128)(4,1)S(1)}, s32[]{:S(2)}) async-start(s8[4718592]{0:T(1024)(128)(4,1)} %bitcast.93), calls=%async_computation.2 | async-start | bytes 8388608
  283.0 5.0 %slice-start.1 = ((s8[4718592]{0:T(1024)(128)(4,1)}), s8[524288]{0:T(1024)(128)(4,1)S(1)}, s32[]{:S(2)}) async-start(s8[4718592]{0:T(1024)(128)(4,1)} %bitcast.93), calls=%async_computation.3 | async-start | bytes 1048576
  289.7 4.7 %copy-start.2 = (f32[4,128,768]{2,1,0:T(8,128)S(1)}, f32[4,128,768]{2,1,0:T(8,128)}, u32[]{:S(2)}) copy-start(f32[4,128,768]{2,1,0:T(8,128)} %fusion.17) | copy-start | bytes 4718596
  294.4 4.4 %copy-start.4 = (f32[4,768,128]{1,2,0:T(8,128)S(1)}, f32[4,768,128]{1,2,0:T(8,128)}, u32[]{:S(2)}) copy-start(f32[4,768,128]{1,2,0:T(8,128)} %fusion.10) | copy-start | bytes 4718596
  299.8 1.2 copy-start.5
Sparse Core Ops, SparseCore 0:
  14.6 95.1 all-gather.6
  113.0 95.4 all-gather.4
where the time goes:
time: 311 us; the launch traced here: 309 us
  waiting for transfers between devices  106 us (34%)
  other arithmetic  72.6 us (23%)
  blocking collectives  69.9 us (22%)
  matrix products  31.2 us (10%)
  between operations  14.9 us (5%)
  local copies, waits for them, and re-layouts  13.4 us (4%)
    all_gather x2, waiting for transfers between devices, prefix(): gathered = jax.tree.map(lambda a: lax.all_gather(a, axis), part)  106 us
    unnamed x1, blocking collectives  69.9 us
    select_n x31, other arithmetic, segment_join(): jnp.where(later[1] > 0.5, later[0], earlier[0] + later[0])  52.4 us
    gt x31, other arithmetic, segment_join(): later[1] > 0.5  18.2 us
    unnamed x34, local copies, waits for them, and re-layouts  9.06 us
  transfers between devices with their start and end apart: 2, of which 2 were waited for; matrix products, arithmetic and copies ran while one was open for 5% of the time, Pallas kernels for 0%

commit v1 on v0

v1 whole, which is shorter than its diff:
```python
import functools

import jax
import jax.numpy as jnp
from jax import lax
from jax.experimental import pallas as pl
from jax.experimental.pallas import tpu as pltpu
from jax.sharding import PartitionSpec as P

MESH = pl.DeviceIdType.MESH
DH = 128
T = 768
NH = 4
DOCS = 16
NX = 4
QT = DH // NX
TB = 256
NB = T // TB
LAST_ROW = 3
REACH = 4
F32 = jnp.float32
BF16 = jnp.bfloat16


def dot_nn(a, b):
    return lax.dot_general(a, b, (((1,), (0,)), ((), ())), preferred_element_type=F32)


def dot_nt(a, b):
    return lax.dot_general(a, b, (((1,), (1,)), ((), ())), preferred_element_type=F32)


def dot_tn(a, b):
    return lax.dot_general(a, b, (((0,), (0,)), ((), ())), preferred_element_type=F32)


def split(a):
    high = a.astype(BF16)
    return high, (a - high.astype(F32)).astype(BF16)


def fused_kernel(
    len_hbm, q_hbm, k_hbm, v_hbm, g_hbm, o_att, o_gq, o_gk, o_gv,
    q, k, v, g, low, pa, pb, pc, pd, loc, p1, zs, zr, p3, st,
    rs_b, head_b, tail_b, tail_low, first_b,
    len_ref, len_sem, in_sem, s1, r1, sz, rz, s3, r3,
):
    seq = lax.axis_index("seq")
    z = seq // NX
    x = seq % NX
    offset = seq * T

    def goes_up(row, d):
        return (row >= 0) & ((row + d <= LAST_ROW) | ((row >= LAST_ROW) & (row + d <= 7)))

    def peer_x(d):
        return {"seq": z * NX + lax.rem(x + d, NX)}

    def peer_z(d):
        return {"seq": (z + d) * NX + x}

    lengths = pltpu.make_async_copy(len_hbm, len_ref, len_sem)
    lengths.start()

    barrier = pltpu.get_barrier_semaphore()
    for d in range(1, NX):
        pl.semaphore_signal(barrier, inc=1, device_id=peer_x(d), device_id_type=MESH)
    for d in range(1, REACH + 1):
        @pl.when(goes_up(z, d))
        def _():
            pl.semaphore_signal(barrier, inc=1, device_id=peer_z(d), device_id_type=MESH)

        @pl.when(goes_up(z - d, d))
        def _():
            pl.semaphore_signal(barrier, inc=1, device_id=peer_z(-d), device_id_type=MESH)

    def fetches(h):
        columns = pl.ds(pl.multiple_of(h * DH, DH), DH)
        return [
            pltpu.make_async_copy(src.at[:, columns], dst.at[h], in_sem.at[h, i])
            for i, (src, dst) in enumerate(((k_hbm, k), (v_hbm, v), (g_hbm, g), (q_hbm, q)))
        ]

    for h in range(NH):
        for copy in fetches(h):
            copy.start()

    lengths.wait()
    starts = [jnp.int32(0)]
    for j in range(DOCS - 1):
        starts.append(starts[-1] + len_ref[j])

    def last_start_before(limit):
        found = jnp.int32(0)
        for j in range(1, DOCS):
            found = jnp.where(starts[j] < limit, starts[j], found)
        return found

    row = z * (NX * T)
    has_start = [
        last_start_before(row + (i + 1) * T) >= row + i * T for i in range(NX)
    ]
    before_row = last_start_before(row)
    up_open = [True] + [before_row < row - (d - 1) * NX * T for d in range(2, REACH + 1)]
    down_open = [True] + [
        last_start_before(row + d * NX * T) < row + NX * T for d in range(2, REACH + 1)
    ]

    def first_of(shape, axis):
        place = lax.broadcasted_iota(jnp.int32, shape, axis)
        first = jnp.full(shape, -offset, jnp.int32)
        for j in range(1, DOCS):
            local = starts[j] - offset
            first = jnp.where(place >= local, local, first)
        return place, first

    place, first = first_of((T, DH), 0)
    scale = lax.rsqrt((place - first + 1).astype(F32) * DH)
    tail_from = last_start_before(offset + T) - offset
    tails = jnp.where(place >= tail_from, 1.0, 0.0)
    first_b[...] = first
    rs_b[...] = scale
    head_b[...] = jnp.where(first < 0, scale, 0.0)
    tail_b[...] = tails
    tail_low[...] = tails.astype(BF16)
    place_r, first_r = first_of((1, T), 1)
    scale_r = lax.rsqrt((place_r - first_r + 1).astype(F32) * DH)

    nz = jnp.where(z == LAST_ROW, 7, jnp.where(z < LAST_ROW, 3, 4))
    pl.semaphore_wait(barrier, NX - 1 + nz)

    def first_copy(h, d):
        target = lax.rem(x + d, NX)
        return pltpu.make_async_remote_copy(
            loc.at[h, :, pl.ds(pl.multiple_of(target * QT, QT), QT), :],
            p1.at[h, x],
            s1.at[h, d],
            r1.at[h, d],
            device_id=peer_x(d),
            device_id_type=MESH,
        )

    def row_copy(h, side, d):
        return pltpu.make_async_remote_copy(
            zs.at[h, side],
            zr.at[h, side, d - 1],
            sz.at[h, side, d - 1],
            rz.at[h, side, d - 1],
            device_id=peer_z(d if side == 0 else -d),
            device_id_type=MESH,
        )

    def last_copy(h, d):
        return pltpu.make_async_remote_copy(
            p3.at[h, lax.rem(x + d, NX)],
            st.at[h, :, pl.ds(pl.multiple_of(x * QT, QT), QT), :],
            s3.at[h, d],
            r3.at[h, d],
            device_id=peer_x(d),
            device_id_type=MESH,
        )

    mine = pl.ds(pl.multiple_of(x * QT, QT), QT)

    def states(h, carry):
        for copy in fetches(h):
            copy.wait()
        loc[h, 0] = dot_tn(k[h], v[h] * tail_low[...])
        gf = g[h].astype(F32)
        low[h] = (rs_b[...] * gf).astype(BF16)
        high_part, low_part = split(head_b[...] * gf)
        both = dot_tn(q[h], jnp.concatenate([high_part, low_part], axis=1))
        loc[h, 1] = both[:, :DH] + both[:, DH:]
        for d in range(1, NX):
            first_copy(h, d).start()
        p1[h, x] = loc[h, :, mine, :]
        return carry

    lax.fori_loop(0, NH, states, 0)

    def forward(h):
        for i in range(NB):
            n = TB * (i + 1)
            rows = pl.ds(TB * i, TB)
            over = lambda a: jnp.concatenate([a] * (n // DH), axis=1)
            s_at = lax.broadcasted_iota(jnp.int32, (TB, n), 1)
            t_at = lax.broadcasted_iota(jnp.int32, (TB, n), 0) + TB * i
            seen = (s_at >= over(first_b[rows, :])) & (s_at <= t_at)
            rs = rs_b[rows, :]
            scores = dot_nt(q[h, rows, :], k[h, :n, :])
            scores_low = jnp.where(seen, scores, 0.0).astype(BF16)
            pa[h, rows, :] = rs * dot_nn(scores_low, v[h, :n, :])
            raw = dot_nt(g[h, rows, :], v[h, :n, :])
            grad_low = jnp.where(seen, raw * over(rs), 0.0).astype(BF16)
            pb[h, rows, :] = dot_nn(grad_low, k[h, :n, :])

    def backward(h):
        for j in range(NB):
            m = T - TB * j
            lo = TB * j
            rows = pl.ds(lo, TB)
            s_at = lax.broadcasted_iota(jnp.int32, (TB, m), 0) + lo
            t_at = lax.broadcasted_iota(jnp.int32, (TB, m), 1) + lo
            seen = (s_at >= first_r[:, lo:]) & (s_at <= t_at)
            scores = dot_nt(k[h, rows, :], q[h, lo:, :])
            scores_low = jnp.where(seen, scores, 0.0).astype(BF16)
            pd[h, rows, :] = dot_nn(scores_low, low[h, lo:, :])
            raw = dot_nt(v[h, rows, :], g[h, lo:, :])
            grad_low = jnp.where(seen, raw * scale_r[:, lo:], 0.0).astype(BF16)
            pc[h, rows, :] = dot_nn(grad_low, q[h, lo:, :])

    def step_rows(h, carry):
        forward(h)
        for d in range(1, NX):
            first_copy(h, d).wait_recv()
        up = p1[h, 0, 0]
        down = p1[h, NX - 1, 1]
        for i in range(1, NX):
            up = p1[h, i, 0] + jnp.where(has_start[i], 0.0, up)
            back = NX - 1 - i
            down = p1[h, back, 1] + jnp.where(has_start[back], 0.0, down)
        zs[h, 0] = up
        zs[h, 1] = down
        for d in range(1, REACH + 1):
            @pl.when(goes_up(z, d))
            def _():
                row_copy(h, 0, d).start()

            @pl.when(goes_up(z - d, d))
            def _():
                row_copy(h, 1, d).start()
        return carry

    lax.fori_loop(0, NH, step_rows, 0)

    def step_last(h, carry):
        backward(h)
        up = jnp.zeros((QT, DH), F32)
        down = jnp.zeros((QT, DH), F32)
        for d in range(1, REACH + 1):
            @pl.when(goes_up(z - d, d))
            def _():
                row_copy(h, 0, d).wait_recv()

            @pl.when(goes_up(z, d))
            def _():
                row_copy(h, 1, d).wait_recv()

            up = up + jnp.where(goes_up(z - d, d) & up_open[d - 1], zr[h, 0, d - 1], 0.0)
            down = down + jnp.where(goes_up(z, d) & down_open[d - 1], zr[h, 1, d - 1], 0.0)
        for i in range(NX):
            p3[h, i, 0] = up
            up = p1[h, i, 0] + jnp.where(has_start[i], 0.0, up)
            back = NX - 1 - i
            p3[h, back, 1] = down
            down = p1[h, back, 1] + jnp.where(has_start[back], 0.0, down)
        for d in range(1, NX):
            last_copy(h, d).start()
        st[h, :, mine, :] = p3[h, x]
        return carry

    lax.fori_loop(0, NH, step_last, 0)

    def finish(h, carry):
        for d in range(1, NX):
            last_copy(h, d).wait_recv()
        kv_high, kv_low = split(st[h, 0])
        qg_high, qg_low = split(st[h, 1])
        columns = pl.ds(pl.multiple_of(h * DH, DH), DH)
        kv_wide = jnp.concatenate([kv_high, kv_low], axis=1)
        kv_tall = jnp.concatenate([kv_high, kv_low], axis=0)
        qg_wide = jnp.concatenate([qg_high, qg_low], axis=1)
        qg_tall = jnp.concatenate([qg_high, qg_low], axis=0)
        for i in range(NB):
            rows = pl.ds(TB * i, TB)
            twice = lambda a: jnp.concatenate([a[h, rows, :]] * 2, axis=1)
            head = head_b[rows, :]
            tail = tail_b[rows, :]
            o_att[rows, columns] = (pa[h, rows, :] + head * dot_nn(twice(q), kv_tall)).astype(BF16)
            o_gq[rows, columns] = (pb[h, rows, :] + head * dot_nt(twice(g), kv_wide)).astype(BF16)
            o_gk[rows, columns] = (pc[h, rows, :] + tail * dot_nt(twice(v), qg_wide)).astype(BF16)
            o_gv[rows, columns] = (pd[h, rows, :] + tail * dot_nn(twice(k), qg_tall)).astype(BF16)
        return carry

    lax.fori_loop(0, NH, finish, 0)

    def drain(h, carry):
        for d in range(1, NX):
            first_copy(h, d).wait_send()
            last_copy(h, d).wait_send()
        for d in range(1, REACH + 1):
            @pl.when(goes_up(z, d))
            def _():
                row_copy(h, 0, d).wait_send()

            @pl.when(goes_up(z - d, d))
            def _():
                row_copy(h, 1, d).wait_send()
        return carry

    lax.fori_loop(0, NH, drain, 0)


def store_kernel(*refs):
    ins, outs, sem = refs[:4], refs[4:8], refs[8]
    copies = [pltpu.make_async_copy(a, b, sem.at[i]) for i, (a, b) in enumerate(zip(ins, outs))]
    for copy in copies:
        copy.start()
    for copy in copies:
        copy.wait()


def per_device(query_rows, key_rows, value_rows, grad_out, doc_lengths):
    whole = pl.BlockSpec(memory_space=pltpu.HBM)
    in_vmem = pl.BlockSpec(memory_space=pltpu.VMEM)
    wide = (T, NH * DH)
    heads = (NH, T, DH)
    dma = pltpu.SemaphoreType.DMA
    results = pl.pallas_call(
        fused_kernel,
        name="attend",
        out_shape=[pltpu.VMEM(wide, BF16)] * 4,
        in_specs=[whole] * 5,
        out_specs=[in_vmem] * 4,
        scratch_shapes=[pltpu.VMEM(heads, BF16)] * 5
        + [pltpu.VMEM(heads, F32)] * 4
        + [
            pltpu.VMEM((NH, 2, DH, DH), F32),
            pltpu.VMEM((NH, NX, 2, QT, DH), F32),
            pltpu.VMEM((NH, 2, QT, DH), F32),
            pltpu.VMEM((NH, 2, REACH, QT, DH), F32),
            pltpu.VMEM((NH, NX, 2, QT, DH), F32),
            pltpu.VMEM((NH, 2, DH, DH), F32),
            pltpu.VMEM((T, DH), F32),
            pltpu.VMEM((T, DH), F32),
            pltpu.VMEM((T, DH), F32),
            pltpu.VMEM((T, DH), BF16),
            pltpu.VMEM((T, DH), jnp.int32),
            pltpu.SMEM((DOCS,), jnp.int32),
            dma,
            dma((NH, 4)),
            dma((NH, NX)),
            dma((NH, NX)),
            dma((NH, 2, REACH)),
            dma((NH, 2, REACH)),
            dma((NH, NX)),
            dma((NH, NX)),
        ],
        compiler_params=pltpu.CompilerParams(
            collective_id=0, has_side_effects=True, vmem_limit_bytes=40 << 20
        ),
    )(*(
        pltpu.with_memory_space_constraint(a, pltpu.HBM)
        for a in (doc_lengths, query_rows, key_rows, value_rows, grad_out)
    ))
    return tuple(
        pl.pallas_call(
            store_kernel,
            name="store",
            out_shape=[jax.ShapeDtypeStruct(wide, BF16)] * 4,
            in_specs=[in_vmem] * 4,
            out_specs=[whole] * 4,
            scratch_shapes=[dma((4,))],
            compiler_params=pltpu.CompilerParams(vmem_limit_bytes=8 << 20),
        )(*results)
    )


def solution(mesh):
    placed = (P("seq", "head"), P("seq", "head"), P("seq", "head"), P("seq", "head"), P())
    return jax.shard_map(
        per_device,
        mesh=mesh,
        in_specs=placed,
        out_specs=(P("seq", "head"), P("seq", "head"), P("seq", "head"), P("seq", "head")),
        check_vma=False,
    )
```

time: 311 us -> 30 us (0.10)
  the two profiles are of different devices: /device:TPU:230 before, /device:TPU:16 now
where the time goes in v1:
time: 30 us; the launch traced here: 29.9 us
  Pallas kernels  29.3 us (98%)
  between operations  0.64 us (2%)
    pallas_call x1, Pallas kernels, per_device(): pl.pallas_call(fused_kernel, name='attend', out_shape=[pltpu.VMEM(wide, B...  27.6 us
    pallas_call x1, Pallas kernels, per_device(): pl.pallas_call(store_kernel, name='store', out_shape=[jax.ShapeDtypeStruc...  1.69 us

profile of v1, /device:TPU:16, one launch (start us, length us, event | category | flops | bytes accessed | tf_op | source)
XLA Modules:
  0.0 29.9 jit_solution(10338363072024465632)
XLA Ops:
  0.6 27.6 %attend.1 = (bf16[768,512]{1,0:T(8,128)(2,1)S(1)}, bf16[768,512]{1,0:T(8,128)(2,1)S(1)}, bf16[768,512]{1,0:T(8,128)(2,1)S(1)}, bf16[768,512]{1,0:T(8,128)(2,1)S(1)}) custom-call(s32[16]{0:T(128)} %len_hbm.1, bf16[768,512]{1,0:T(8,128)(2,1)} %q_hbm.1, bf16[768,512]{1,0:T(8,128)(2,1)} %k_hbm.1, bf16[768,512]{1,0:T(8,128)(2,1)} %v_hbm.1, bf16[768,512]{1,0:T(8,128)(2,1)} %g_hbm.1), custom_call_target="tpu_custom_call" | custom-call | tf_op jit(solution)/shard_map/attend/pallas_call | solution.py:319
  28.2 1.7 %store.1 = (bf16[768,512]{1,0:T(8,128)(2,1)}, bf16[768,512]{1,0:T(8,128)(2,1)}, bf16[768,512]{1,0:T(8,128)(2,1)}, bf16[768,512]{1,0:T(8,128)(2,1)}) custom-call(bf16[768,512]{1,0:T(8,128)(2,1)S(1)} %get-tuple-element.8.refs_0_, bf16[768,512]{1,0:T(8,128)(2,1)S(1)} %get-tuple-element.9.refs_1_, bf16[768,512]{1,0:T(8,128)(2,1)S(1)} %get-tuple-element.10.refs_2_, ...), custom_call_target="tpu_custom_call" | custom-call | tf_op jit(solution)/shard_map/store/pallas_call | solution.py:357

commit v2 on v1

v2 whole, which is shorter than its diff:
```python
import functools

import jax
import jax.numpy as jnp
from jax import lax
from jax.experimental import pallas as pl
from jax.experimental.pallas import tpu as pltpu
from jax.sharding import PartitionSpec as P

MESH = pl.DeviceIdType.MESH
DH = 128
T = 768
NH = 4
DOCS = 16
NX = 4
QT = DH // NX
TB = 256
NB = T // TB
FIRST = 2
FAR_FIRST = (2, 1, 3)
LAST_ROW = 3
NG = 4
F32 = jnp.float32
BF16 = jnp.bfloat16


def dot_nn(a, b):
    return lax.dot_general(a, b, (((1,), (0,)), ((), ())), preferred_element_type=F32)


def dot_nt(a, b):
    return lax.dot_general(a, b, (((1,), (1,)), ((), ())), preferred_element_type=F32)


def dot_tn(a, b):
    return lax.dot_general(a, b, (((0,), (0,)), ((), ())), preferred_element_type=F32)


def split(a):
    high = a.astype(BF16)
    return high, (a - high.astype(F32)).astype(BF16)


def fused_kernel(
    len_hbm, q_hbm, k_hbm, v_hbm, g_hbm, o_att, o_gq, o_gk, o_gv,
    ins, low, pa, pb, pc, pd, kvs, qgs, loc, p1, zs, zr, zx, p3, st,
    rs_b, head_b, tail_b, tail_low, first_b,
    len_ref, len_sem, above_sem, in_sem, s1, r1, sz, rz, sx, rx, sw, rw, s3, s3_part, r3,
):
    q, k, v, g = (ins.at[:, i] for i in range(4))
    seq = lax.axis_index("seq")
    z = seq // NX
    x = seq % NX
    offset = seq * T
    base = (z // NG) * NG
    r = z - base
    below = z == NG - 1
    above = z == NG
    begins = below & (x >= NX - 2)

    def peer_x(d):
        return {"seq": z * NX + lax.rem(x + d, NX)}

    def peer_row(d):
        return lax.rem(r + d, NG)

    def peer_z(d):
        return {"seq": (base + peer_row(d)) * NX + x}

    def wait_bytes(ref, sem):
        pltpu.make_async_copy(ref, ref, sem).wait()

    lengths = pltpu.make_async_copy(len_hbm, len_ref, len_sem)
    lengths.start()

    barrier = pltpu.get_barrier_semaphore()
    for d in range(1, NX):
        pl.semaphore_signal(barrier, inc=1, device_id=peer_x(d), device_id_type=MESH)
    for d in range(1, NG):
        @pl.when(peer_row(d) > r)
        def _():
            pl.semaphore_signal(barrier, inc=1, device_id=peer_z(d), device_id_type=MESH)

    @pl.when(below)
    def _():
        up = {"seq": NG * NX + x}
        pl.semaphore_signal(barrier, inc=1, device_id=up, device_id_type=MESH)

    @pl.when(begins)
    def _():
        for d in range(1, NX):
            beside = {"seq": NG * NX + lax.rem(x + d, NX)}
            pl.semaphore_signal(barrier, inc=1, device_id=beside, device_id_type=MESH)

    def fetches(h):
        columns = pl.ds(pl.multiple_of(h * DH, DH), DH)
        return [
            pltpu.make_async_copy(src.at[:, columns], ins.at[h, i], in_sem.at[h])
            for i, src in enumerate((q_hbm, k_hbm, v_hbm, g_hbm))
        ]

    for h in range(NH):
        for copy in fetches(h):
            copy.start()

    lengths.wait()
    starts = [jnp.int32(0)]
    for j in range(DOCS - 1):
        starts.append(starts[-1] + len_ref[j])

    def last_start_before(limit):
        found = jnp.int32(0)
        for j in range(1, DOCS):
            found = jnp.where(starts[j] < limit, starts[j], found)
        return found

    row = z * (NX * T)
    has_start = [
        last_start_before(row + (i + 1) * T) >= row + i * T for i in range(NX)
    ]
    before_row = last_start_before(row)
    up_open = [before_row < (base + i + 1) * NX * T for i in range(NG)]
    down_open = [last_start_before((base + i) * NX * T) < row + NX * T for i in range(NG)]

    def first_of(place):
        first = jnp.full(place.shape, -offset, jnp.int32)
        for j in range(1, DOCS):
            local = starts[j] - offset
            first = jnp.where(place >= local, local, first)
        return first, lax.rsqrt((place - first + 1).astype(F32) * DH)

    chunk_start = []
    for c in range(NB):
        from_here = last_start_before(offset + TB * (c + 1)) - offset
        chunk_start.append(from_here >= TB * c)
        for top in range(TB * c, TB * (c + 1), DH):
            rows = pl.ds(top, DH)
            place = lax.broadcasted_iota(jnp.int32, (DH, DH), 0) + top
            first, scale = first_of(place)
            first_b[rows, :] = first
            rs_b[rows, :] = scale
            head_b[rows, :] = jnp.where(first < TB * c, scale, 0.0)
            tails = jnp.where(place >= from_here, 1.0, 0.0)
            tail_b[rows, :] = tails
            tail_low[rows, :] = tails.astype(BF16)

    from_below = jnp.where(above, jnp.where(x >= NX - 2, 2, 3), r)
    pl.semaphore_wait(barrier, NX - 1 + from_below)
    for d in range(1, NG):
        @pl.when(peer_row(d) < r)
        def _():
            pl.semaphore_signal(above_sem, inc=1, device_id=peer_z(d), device_id_type=MESH)

    @pl.when(above)
    def _():
        down = {"seq": (NG - 1) * NX + x}
        pl.semaphore_signal(above_sem, inc=1, device_id=down, device_id_type=MESH)

    def first_copy(h, d):
        target = lax.rem(x + d, NX)
        return pltpu.make_async_remote_copy(
            loc.at[h, :, pl.ds(pl.multiple_of(target * QT, QT), QT), :],
            p1.at[h, x],
            s1,
            r1.at[h],
            device_id=peer_x(d),
            device_id_type=MESH,
        )

    def row_copy(h, d):
        return pltpu.make_async_remote_copy(
            zs.at[h, jnp.where(peer_row(d) > r, 1, 0)],
            zr.at[h, r],
            sz,
            rz.at[h],
            device_id=peer_z(d),
            device_id_type=MESH,
        )

    def over_copy(h):
        return pltpu.make_async_remote_copy(
            zs.at[h, 1:3],
            zx.at[h],
            sx,
            rx.at[h],
            device_id={"seq": NG * NX + x},
            device_id_type=MESH,
        )

    def under_copy(h, i):
        return pltpu.make_async_remote_copy(
            zx.at[h, i],
            st.at[h, 1, mine, :],
            sw,
            rw.at[h],
            device_id={"seq": (NG - 1) * NX + NX - 2 + i},
            device_id_type=MESH,
        )

    def last_copy(h, d):
        return pltpu.make_async_remote_copy(
            p3.at[h, lax.rem(x + d, NX)],
            st.at[h, :, mine, :],
            s3,
            r3.at[h],
            device_id=peer_x(d),
            device_id_type=MESH,
        )

    def last_part(h, d):
        return pltpu.make_async_remote_copy(
            p3.at[h, lax.rem(x + d, NX), 0],
            st.at[h, 0, mine, :],
            s3_part,
            r3.at[h],
            device_id=peer_x(d),
            device_id_type=MESH,
        )

    mine = pl.ds(pl.multiple_of(x * QT, QT), QT)

    def states(h, carry):
        wait_bytes(ins.at[h], in_sem.at[h])
        for c in range(NB):
            rows = pl.ds(TB * c, TB)
            kvs[h, c] = dot_tn(k[h, rows, :], v[h, rows, :] * tail_low[rows, :])
            gf = g[h, rows, :].astype(F32)
            low[h, rows, :] = (rs_b[rows, :] * gf).astype(BF16)
            high_part, low_part = split(head_b[rows, :] * gf)
            both = dot_tn(q[h, rows, :], jnp.concatenate([high_part, low_part], axis=1))
            qgs[h, c] = both[:, :DH] + both[:, DH:]
        up = kvs[h, 0]
        down = qgs[h, NB - 1]
        for c in range(1, NB):
            up = kvs[h, c] + jnp.where(chunk_start[c], 0.0, up)
            back = NB - 1 - c
            down = qgs[h, back] + jnp.where(chunk_start[back], 0.0, down)
        loc[h, 0] = up
        loc[h, 1] = down
        for d in FAR_FIRST:
            first_copy(h, d).start()
        p1[h, x] = loc[h, :, mine, :]
        return carry

    lax.fori_loop(0, NH, states, 0)

    def inside(h):
        for c in range(NB):
            rows = pl.ds(TB * c, TB)
            qc, kc, vc, gc = (a[h, rows, :] for a in (q, k, v, g))
            over = lambda a: jnp.concatenate([a] * (TB // DH), axis=1)
            high = lax.broadcasted_iota(jnp.int32, (TB, TB), 0)
            wide = lax.broadcasted_iota(jnp.int32, (TB, TB), 1)
            seen = (wide + TB * c >= over(first_b[rows, :])) & (wide <= high)
            rs = rs_b[rows, :]
            scores = jnp.where(seen, dot_nt(qc, kc), 0.0).astype(BF16)
            grads = jnp.where(seen, dot_nt(gc, vc) * over(rs), 0.0).astype(BF16)
            pa[h, rows, :] = rs * dot_nn(scores, vc)
            pb[h, rows, :] = dot_nn(grads, kc)
            pd[h, rows, :] = dot_tn(scores, low[h, rows, :])
            pc[h, rows, :] = dot_tn(grads, qc)

    def step_rows(h, carry):
        wait_bytes(p1.at[h, 1:], r1.at[h])
        up = p1[h, 0, 0]
        down = p1[h, NX - 1, 1]
        for i in range(1, NX):
            up = p1[h, i, 0] + jnp.where(has_start[i], 0.0, up)
            back = NX - 1 - i
            down = p1[h, back, 1] + jnp.where(has_start[back], 0.0, down)
        zs[h, 0] = down
        zs[h, 1] = up
        zs[h, 2] = p1[h, NX - 1, 1]

        @pl.when(below)
        def _():
            over_copy(h).start()

        @pl.when(above)
        def _():
            wait_bytes(zx.at[h], rx.at[h])
            zs[h, 1] = zs[h, 1] + zx[h, 0]

        for d in range(1, NG):
            row_copy(h, d).start()
        return carry

    def inner(h, carry):
        inside(h)
        return carry

    lax.fori_loop(0, FIRST, inner, 0)

    @pl.when(below | (r < NG - 1))
    def _():
        pl.semaphore_wait(above_sem, NG - 1 - r + jnp.where(below, 1, 0))

    lax.fori_loop(0, NH, step_rows, 0)
    lax.fori_loop(FIRST, NH, inner, 0)

    def step_last(h, carry):
        wait_bytes(zr.at[h, 1:], rz.at[h])
        up = jnp.where(above, zx[h, 0], 0.0)
        down = jnp.zeros((QT, DH), F32)
        for i in range(NG):
            up = up + jnp.where((r > i) & up_open[i], zr[h, i], 0.0)
            down = down + jnp.where((r < i) & down_open[i], zr[h, i], 0.0)
        for i in range(NX):
            p3[h, i, 0] = up
            up = p1[h, i, 0] + jnp.where(has_start[i], 0.0, up)
            back = NX - 1 - i
            p3[h, back, 1] = down
            down = p1[h, back, 1] + jnp.where(has_start[back], 0.0, down)

        @pl.when(above)
        def _():
            zx[h, 0] = down + zx[h, 1]
            zx[h, 1] = down
            for i in range(2):
                under_copy(h, i).start()

        for d in FAR_FIRST:
            part = below & (lax.rem(x + d, NX) >= NX - 2)

            @pl.when(~part)
            def _():
                last_copy(h, d).start()

            @pl.when(part)
            def _():
                last_part(h, d).start()

        st[h, 0, mine, :] = p3[h, x, 0]

        @pl.when(~begins)
        def _():
            st[h, 1, mine, :] = p3[h, x, 1]

        return carry

    lax.fori_loop(0, NH, step_last, 0)

    wait_bytes(p1.at[:, 1:], s1)
    wait_bytes(zr.at[:, 1:], sz)

    @pl.when(below)
    def _():
        wait_bytes(zx, sx)

    def finish(h, carry):
        @pl.when(begins)
        def _():
            wait_bytes(p3.at[h, 1:, 0], r3.at[h])
            wait_bytes(st.at[h, 1], rw.at[h])

        @pl.when(~begins)
        def _():
            wait_bytes(p3.at[h, 1:], r3.at[h])

        columns = pl.ds(pl.multiple_of(h * DH, DH), DH)
        kv_in = [st[h, 0]]
        for c in range(NB - 1):
            kv_in.append(kvs[h, c] + jnp.where(chunk_start[c], 0.0, kv_in[-1]))
        qg_in = [st[h, 1]]
        for c in range(NB - 1, 0, -1):
            qg_in.insert(0, qgs[h, c] + jnp.where(chunk_start[c], 0.0, qg_in[0]))
        for c in range(NB):
            rows = pl.ds(TB * c, TB)
            kv_parts = split(kv_in[c])
            qg_parts = split(qg_in[c])
            kv_wide, kv_tall = (jnp.concatenate(kv_parts, axis=i) for i in (1, 0))
            qg_wide, qg_tall = (jnp.concatenate(qg_parts, axis=i) for i in (1, 0))
            twice = lambda a: jnp.concatenate([a[h, rows, :]] * 2, axis=1)
            head = head_b[rows, :]
            tail = tail_b[rows, :]
            o_att[rows, columns] = (pa[h, rows, :] + head * dot_nn(twice(q), kv_tall)).astype(BF16)
            o_gq[rows, columns] = (pb[h, rows, :] + head * dot_nt(twice(g), kv_wide)).astype(BF16)
            o_gk[rows, columns] = (pc[h, rows, :] + tail * dot_nt(twice(v), qg_wide)).astype(BF16)
            o_gv[rows, columns] = (pd[h, rows, :] + tail * dot_nn(twice(k), qg_tall)).astype(BF16)
        return carry

    lax.fori_loop(0, NH, finish, 0)

    @pl.when(~below)
    def _():
        wait_bytes(p3.at[:, 1:], s3)

    @pl.when(begins)
    def _():
        wait_bytes(p3.at[:, 2:], s3)
        wait_bytes(p3.at[:, 0, 0], s3_part)

    @pl.when(below & ~begins)
    def _():
        wait_bytes(p3.at[:, 0], s3)
        wait_bytes(p3.at[:, 2:, 0], s3_part)

    @pl.when(above)
    def _():
        wait_bytes(zx, sw)


def store_kernel(*refs):
    ins, outs, sem = refs[:4], refs[4:8], refs[8]
    copies = [pltpu.make_async_copy(a, b, sem.at[i]) for i, (a, b) in enumerate(zip(ins, outs))]
    for copy in copies:
        copy.start()
    for copy in copies:
        copy.wait()


def per_device(query_rows, key_rows, value_rows, grad_out, doc_lengths):
    whole = pl.BlockSpec(memory_space=pltpu.HBM)
    in_vmem = pl.BlockSpec(memory_space=pltpu.VMEM)
    wide = (T, NH * DH)
    heads = (NH, T, DH)
    dma = pltpu.SemaphoreType.DMA
    results = pl.pallas_call(
        fused_kernel,
        name="attend",
        out_shape=[pltpu.VMEM(wide, BF16)] * 4,
        in_specs=[whole] * 5,
        out_specs=[in_vmem] * 4,
        scratch_shapes=[pltpu.VMEM((NH, 4, T, DH), BF16), pltpu.VMEM(heads, BF16)]
        + [pltpu.VMEM(heads, F32)] * 4
        + [
            pltpu.VMEM((NH, NB, DH, DH), F32),
            pltpu.VMEM((NH, NB, DH, DH), F32),
            pltpu.VMEM((NH, 2, DH, DH), F32),
            pltpu.VMEM((NH, NX, 2, QT, DH), F32),
            pltpu.VMEM((NH, 3, QT, DH), F32),
            pltpu.VMEM((NH, NG, QT, DH), F32),
            pltpu.VMEM((NH, 2, QT, DH), F32),
            pltpu.VMEM((NH, NX, 2, QT, DH), F32),
            pltpu.VMEM((NH, 2, DH, DH), F32),
            pltpu.VMEM((T, DH), F32),
            pltpu.VMEM((T, DH), F32),
            pltpu.VMEM((T, DH), F32),
            pltpu.VMEM((T, DH), BF16),
            pltpu.VMEM((T, DH), jnp.int32),
            pltpu.SMEM((DOCS,), jnp.int32),
            dma,
            pltpu.SemaphoreType.REGULAR,
            dma((NH,)),
            dma,
            dma((NH,)),
            dma,
            dma((NH,)),
            dma,
            dma((NH,)),
            dma,
            dma((NH,)),
            dma,
            dma,
            dma((NH,)),
        ],
        compiler_params=pltpu.CompilerParams(
            collective_id=0, has_side_effects=True, vmem_limit_bytes=40 << 20
        ),
    )(*(
        pltpu.with_memory_space_constraint(a, pltpu.HBM)
        for a in (doc_lengths, query_rows, key_rows, value_rows, grad_out)
    ))
    return tuple(
        pl.pallas_call(
            store_kernel,
            name="store",
            out_shape=[jax.ShapeDtypeStruct(wide, BF16)] * 4,
            in_specs=[in_vmem] * 4,
            out_specs=[whole] * 4,
            scratch_shapes=[dma((4,))],
            compiler_params=pltpu.CompilerParams(vmem_limit_bytes=8 << 20),
        )(*results)
    )


def solution(mesh):
    placed = (P("seq", "head"), P("seq", "head"), P("seq", "head"), P("seq", "head"), P())
    return jax.shard_map(
        per_device,
        mesh=mesh,
        in_specs=placed,
        out_specs=(P("seq", "head"), P("seq", "head"), P("seq", "head"), P("seq", "head")),
        check_vma=False,
    )
```

time: 30 us -> 25.5 us (0.85)
  the two profiles are of different devices: /device:TPU:16 before, /device:TPU:136 now
where the time goes in v2:
time: 25.5 us; the launch traced here: 25.4 us
  Pallas kernels  24.8 us (97%)
  between operations  0.64 us (3%)
    pallas_call x1, Pallas kernels, per_device(): pl.pallas_call(fused_kernel, name='attend', out_shape=[pltpu.VMEM(wide, B...  23.1 us
    pallas_call x1, Pallas kernels, per_device(): pl.pallas_call(store_kernel, name='store', out_shape=[jax.ShapeDtypeStruc...  1.69 us

profile of v2, /device:TPU:136, one launch (start us, length us, event | category | flops | bytes accessed | tf_op | source)
XLA Modules:
  0.0 25.4 jit_solution(15284345584948266166)
XLA Ops:
  0.6 23.1 %attend.1 = (bf16[768,512]{1,0:T(8,128)(2,1)S(1)}, bf16[768,512]{1,0:T(8,128)(2,1)S(1)}, bf16[768,512]{1,0:T(8,128)(2,1)S(1)}, bf16[768,512]{1,0:T(8,128)(2,1)S(1)}) custom-call(s32[16]{0:T(128)} %len_hbm.1, bf16[768,512]{1,0:T(8,128)(2,1)} %q_hbm.1, bf16[768,512]{1,0:T(8,128)(2,1)} %k_hbm.1, bf16[768,512]{1,0:T(8,128)(2,1)} %v_hbm.1, bf16[768,512]{1,0:T(8,128)(2,1)} %g_hbm.1), custom_call_target="tpu_custom_call" | custom-call | tf_op jit(solution)/shard_map/attend/pallas_call | solution.py:418
  23.7 1.7 %store.1 = (bf16[768,512]{1,0:T(8,128)(2,1)}, bf16[768,512]{1,0:T(8,128)(2,1)}, bf16[768,512]{1,0:T(8,128)(2,1)}, bf16[768,512]{1,0:T(8,128)(2,1)}) custom-call(bf16[768,512]{1,0:T(8,128)(2,1)S(1)} %get-tuple-element.8.refs_0_, bf16[768,512]{1,0:T(8,128)(2,1)S(1)} %get-tuple-element.9.refs_1_, bf16[768,512]{1,0:T(8,128)(2,1)S(1)} %get-tuple-element.10.refs_2_, ...), custom_call_target="tpu_custom_call" | custom-call | tf_op jit(solution)/shard_map/store/pallas_call | solution.py:465

commit v3 on v2

--- a/solution.py
+++ b/solution.py
@@ -16,7 +16,7 @@
 QT = DH // NX
 TB = 256
 NB = T // TB
-FIRST = 2
+FIRST = 3
 FAR_FIRST = (2, 1, 3)
 LAST_ROW = 3
 NG = 4
@@ -296,7 +296,6 @@
         pl.semaphore_wait(above_sem, NG - 1 - r + jnp.where(below, 1, 0))
 
     lax.fori_loop(0, NH, step_rows, 0)
-    lax.fori_loop(FIRST, NH, inner, 0)
 
     def step_last(h, carry):
         wait_bytes(zr.at[h, 1:], rz.at[h])
@@ -339,6 +338,7 @@
         return carry
 
     lax.fori_loop(0, NH, step_last, 0)
+    lax.fori_loop(FIRST, NH, inner, 0)
 
     wait_bytes(p1.at[:, 1:], s1)
     wait_bytes(zr.at[:, 1:], sz)

time: 25.5 us -> 24.6 us (0.965)
  the two profiles are of different devices: /device:TPU:136 before, /device:TPU:16 now
where the time goes in v3:
time: 24.6 us; the launch traced here: 24.5 us
  Pallas kernels  23.9 us (97%)
  between operations  0.64 us (3%)
    pallas_call x1, Pallas kernels, per_device(): pl.pallas_call(fused_kernel, name='attend', out_shape=[pltpu.VMEM(wide, B...  22.2 us
    pallas_call x1, Pallas kernels, per_device(): pl.pallas_call(store_kernel, name='store', out_shape=[jax.ShapeDtypeStruc...  1.69 us

profile of v3, /device:TPU:16, one launch (start us, length us, event | category | flops | bytes accessed | tf_op | source)
XLA Modules:
  0.0 24.5 jit_solution(17741769841556330442)
XLA Ops:
  0.6 22.2 %attend.1 = (bf16[768,512]{1,0:T(8,128)(2,1)S(1)}, bf16[768,512]{1,0:T(8,128)(2,1)S(1)}, bf16[768,512]{1,0:T(8,128)(2,1)S(1)}, bf16[768,512]{1,0:T(8,128)(2,1)S(1)}) custom-call(s32[16]{0:T(128)} %len_hbm.1, bf16[768,512]{1,0:T(8,128)(2,1)} %q_hbm.1, bf16[768,512]{1,0:T(8,128)(2,1)} %k_hbm.1, bf16[768,512]{1,0:T(8,128)(2,1)} %v_hbm.1, bf16[768,512]{1,0:T(8,128)(2,1)} %g_hbm.1), custom_call_target="tpu_custom_call" | custom-call | tf_op jit(solution)/shard_map/attend/pallas_call | solution.py:418
  22.8 1.7 %store.1 = (bf16[768,512]{1,0:T(8,128)(2,1)}, bf16[768,512]{1,0:T(8,128)(2,1)}, bf16[768,512]{1,0:T(8,128)(2,1)}, bf16[768,512]{1,0:T(8,128)(2,1)}) custom-call(bf16[768,512]{1,0:T(8,128)(2,1)S(1)} %get-tuple-element.8.refs_0_, bf16[768,512]{1,0:T(8,128)(2,1)S(1)} %get-tuple-element.9.refs_1_, bf16[768,512]{1,0:T(8,128)(2,1)S(1)} %get-tuple-element.10.refs_2_, ...), custom_call_target="tpu_custom_call" | custom-call | tf_op jit(solution)/shard_map/store/pallas_call | solution.py:465

commit v4 on v3

--- a/solution.py
+++ b/solution.py
@@ -43,7 +43,7 @@
 
 def fused_kernel(
     len_hbm, q_hbm, k_hbm, v_hbm, g_hbm, o_att, o_gq, o_gk, o_gv,
-    ins, low, pa, pb, pc, pd, kvs, qgs, loc, p1, zs, zr, zx, p3, st,
+    ins, pa, pb, pc, pd, kvs, qgs, loc, p1, zs, zr, zx, p3, st,
     rs_b, head_b, tail_b, tail_low, first_b,
     len_ref, len_sem, above_sem, in_sem, s1, r1, sz, rz, sx, rx, sw, rw, s3, s3_part, r3,
 ):
@@ -225,7 +225,6 @@
             rows = pl.ds(TB * c, TB)
             kvs[h, c] = dot_tn(k[h, rows, :], v[h, rows, :] * tail_low[rows, :])
             gf = g[h, rows, :].astype(F32)
-            low[h, rows, :] = (rs_b[rows, :] * gf).astype(BF16)
             high_part, low_part = split(head_b[rows, :] * gf)
             both = dot_tn(q[h, rows, :], jnp.concatenate([high_part, low_part], axis=1))
             qgs[h, c] = both[:, :DH] + both[:, DH:]
@@ -257,7 +256,8 @@
             grads = jnp.where(seen, dot_nt(gc, vc) * over(rs), 0.0).astype(BF16)
             pa[h, rows, :] = rs * dot_nn(scores, vc)
             pb[h, rows, :] = dot_nn(grads, kc)
-            pd[h, rows, :] = dot_tn(scores, low[h, rows, :])
+            low = (rs * gc.astype(F32)).astype(BF16)
+            pd[h, rows, :] = dot_tn(scores, low)
             pc[h, rows, :] = dot_tn(grads, qc)
 
     def step_rows(h, carry):
@@ -421,7 +421,7 @@
         out_shape=[pltpu.VMEM(wide, BF16)] * 4,
         in_specs=[whole] * 5,
         out_specs=[in_vmem] * 4,
-        scratch_shapes=[pltpu.VMEM((NH, 4, T, DH), BF16), pltpu.VMEM(heads, BF16)]
+        scratch_shapes=[pltpu.VMEM((NH, 4, T, DH), BF16)]
         + [pltpu.VMEM(heads, F32)] * 4
         + [
             pltpu.VMEM((NH, NB, DH, DH), F32),

time: 24.6 us -> 24.6 us (level)
  no operation moved by 1% of the time
where the time goes in v4:
time: 24.6 us; the launch traced here: 24.5 us
  Pallas kernels  23.9 us (97%)
  between operations  0.64 us (3%)
    pallas_call x1, Pallas kernels, per_device(): pl.pallas_call(fused_kernel, name='attend', out_shape=[pltpu.VMEM(wide, B...  22.2 us
    pallas_call x1, Pallas kernels, per_device(): pl.pallas_call(store_kernel, name='store', out_shape=[jax.ShapeDtypeStruc...  1.69 us

profile of v4, /device:TPU:16, one launch (start us, length us, event | category | flops | bytes accessed | tf_op | source)
XLA Modules:
  0.0 24.5 jit_solution(8011031279102584926)
XLA Ops:
  0.6 22.2 %attend.1 = (bf16[768,512]{1,0:T(8,128)(2,1)S(1)}, bf16[768,512]{1,0:T(8,128)(2,1)S(1)}, bf16[768,512]{1,0:T(8,128)(2,1)S(1)}, bf16[768,512]{1,0:T(8,128)(2,1)S(1)}) custom-call(s32[16]{0:T(128)} %len_hbm.1, bf16[768,512]{1,0:T(8,128)(2,1)} %q_hbm.1, bf16[768,512]{1,0:T(8,128)(2,1)} %k_hbm.1, bf16[768,512]{1,0:T(8,128)(2,1)} %v_hbm.1, bf16[768,512]{1,0:T(8,128)(2,1)} %g_hbm.1), custom_call_target="tpu_custom_call" | custom-call | tf_op jit(solution)/shard_map/attend/pallas_call | solution.py:418
  22.8 1.7 %store.1 = (bf16[768,512]{1,0:T(8,128)(2,1)}, bf16[768,512]{1,0:T(8,128)(2,1)}, bf16[768,512]{1,0:T(8,128)(2,1)}, bf16[768,512]{1,0:T(8,128)(2,1)}) custom-call(bf16[768,512]{1,0:T(8,128)(2,1)S(1)} %get-tuple-element.8.refs_0_, bf16[768,512]{1,0:T(8,128)(2,1)S(1)} %get-tuple-element.9.refs_1_, bf16[768,512]{1,0:T(8,128)(2,1)S(1)} %get-tuple-element.10.refs_2_, ...), custom_call_target="tpu_custom_call" | custom-call | tf_op jit(solution)/shard_map/store/pallas_call | solution.py:465
